TPU v7x, 128 devices: a whole 4x4x4 slice. The times are simulated.
128 devices in a mesh: chan: 16 (over y, z), pair: 8 (over x, core).
Axes of the slice: x: 4, y: 4, z: 4, core: 2. Of those that a mesh axis runs over, the one named last changes fastest.
Arguments:
- eta_blocks: bfloat16 [16, 2048, 2048], P('chan', 'pair'), may hold values from -6 to 6
- omega_blocks: bfloat16 [16, 2048, 2048], P('chan', 'pair'), may hold values from -0.125 to 0.125
- recouple: bfloat16 [16, 2048, 2048], P('chan'), may hold values from -0.125 to 0.125
- block_states: int32 [16], P('chan'), may hold values from 256 to 2048, as said below
- cross_map: int32 [16, 8], P('chan'), may hold values from 0 to 15, all different within a row
- cross_coef: float32 [16, 8], P('chan'), may hold values from -1 to 1
Outputs:
- pair_comm: bfloat16 [16, 2048, 2048], P('chan', 'pair')
- cross_comm: bfloat16 [16, 2048, 2048], P('chan', 'pair')
Inputs may be any that keep to these rules, and one draw needn't show every extreme that they name: `block_states`: each channel has 256 to 2048 live states; channel 0 has all 2048 states live.
All inputs are finite; a program needn't handle non-finite values.
Results may differ from a plain program's by a relative error of at most 0.014.
Values may be sent and summed in bfloat16 or wider, within the bound.
A program may use at most 192 MiB of HBM per device.

v0:
```python
import jax
import jax.numpy as jnp
from jax import lax
from jax.sharding import PartitionSpec as P


def body(eta_blocks, omega_blocks, recouple, block_states, cross_map, cross_coef):
    owned = eta_blocks.shape[0]
    row_count = eta_blocks.shape[1]
    states = eta_blocks.shape[2]
    total_ch = owned * lax.axis_size("chan")
    first_row = lax.axis_index("pair") * row_count
    row_index = first_row + jnp.arange(row_count, dtype=jnp.int32)
    col_index = jnp.arange(states, dtype=jnp.int32)
    limits = block_states[:, None, None]
    live = (row_index[None, :, None] < limits) & (col_index[None, None, :] < limits)
    zero_bf = jnp.zeros((), jnp.bfloat16)
    eta_m = jnp.where(live, eta_blocks, zero_bf)
    omega_m = jnp.where(live, omega_blocks, zero_bf)
    full_eta, full_omega = (
        lax.all_gather(eta_m, "pair", axis=1, tiled=True),
        lax.all_gather(omega_m, "pair", axis=1, tiled=True),
    )
    pair_part = jnp.einsum("cij,cjk->cik", eta_m, full_omega, preferred_element_type=jnp.float32)
    pair_part = pair_part - jnp.einsum(
        "cij,cjk->cik", omega_m, full_eta, preferred_element_type=jnp.float32
    )
    pair_comm = pair_part.astype(jnp.bfloat16)
    eta_cross = jnp.einsum(
        "cij,cjk->cik", eta_m, recouple, preferred_element_type=jnp.float32
    ).astype(jnp.bfloat16)
    omega_cross = jnp.einsum(
        "cij,cjk->cik", omega_m, recouple, preferred_element_type=jnp.float32
    ).astype(jnp.bfloat16)
    omega_full = lax.all_gather(omega_cross, "pair", axis=1, tiled=True)
    product = jnp.einsum("cij,ckj->cik", eta_cross, omega_full, preferred_element_type=jnp.float32)
    targets = jnp.arange(total_ch, dtype=jnp.int32)
    weighing = jnp.sum(
        cross_coef[:, :, None]
        * (cross_map[:, :, None] == targets[None, None, :]).astype(jnp.float32),
        axis=1,
    )
    summed = weighing[0][:, None, None] * product[0][None]
    cross_sum = lax.psum_scatter(
        summed.astype(jnp.bfloat16), "chan", scatter_dimension=0, tiled=True
    )
    return (pair_comm, cross_sum)


def solution(mesh):
    placed = (
        P("chan", "pair", None),
        P("chan", "pair", None),
        P("chan", None, None),
        P("chan"),
        P("chan", None),
        P("chan", None),
    )
    return jax.shard_map(
        body,
        mesh=mesh,
        in_specs=placed,
        out_specs=(P("chan", "pair", None), P("chan", "pair", None)),
        check_vma=False,
    )
```

profile of v0, /device:TPU:1, one launch (start us, length us, event | category | flops | bytes accessed | tf_op | source)
XLA Modules:
  0.0 296.0 jit_solution(5348133827567153892)
XLA Ops:
  7.2 0.0 all-gather.9.cloned.1.call-start
  7.9 3.2 %and_select_fusion = (bf16[1,256,2048]{2,1,0:T(8,128)(2,1)S(1)}, bf16[1,256,2048]{2,1,0:T(8,128)(2,1)}) fusion(bf16[1,256,2048]{2,1,0:T(8,128)(2,1)} %param.7, pred[2048]{0:T(1024)(128)(4,1)S(1)} %iota_compare_fusion, pred[256]{0:T(512)(128)(4,1)S(1)} %add_compare_fusion, bf16[1,256,2048]{2,1,0:T(8,128)(2,1)} %param.6), kind=kLoop, calls=%fused_computation.9 | loop fusion | flops 1572864 | bytes 4196608 | tf_op jit(solution)/shard_map/jit(_where)/select_n | solution.py:19
  11.1 7.1 %fusion.17 = bf16[256,2048]{1,0:T(8,128)(2,1)} fusion(bf16[1,2048,2048]{2,1,0:T(8,128)(2,1)} %param.8, bf16[1,256,2048]{2,1,0:T(8,128)(2,1)S(1)} %get-tuple-element.2), kind=kOutput, calls=%fused_computation.14 | convolution fusion | flops 2148007936 | bytes 10485760 | tf_op jit(solution)/shard_map/cij,cjk->cik/dot_general | solution.py:32
  18.2 0.0 copy-done.1
  18.2 0.0 all-gather.9.cloned.1.call-update
  18.2 0.0 all-gather.7.cloned.1.call-start
  18.2 0.7 all-gather.7.cloned.1.call-update
  19.0 0.0 all-gather.5.cloned.1.call-start
  19.0 0.7 all-gather.5.cloned.1.call-update
  19.7 0.0 reduce-scatter.4.cloned.1.call-start
  19.7 0.0 copy-done.3
  19.7 0.0 copy-done.4
  19.8 0.1 select_reduce_fusion
  19.8 51.8 %all-gather.9.cloned.1.call-done = bf16[2048,2048]{1,0:T(8,128)(2,1)} async-done(((bf16[256,2048]{1,0:T(8,128)(2,1)}), bf16[2048,2048]{1,0:T(8,128)(2,1)}) %all-gather.9.cloned.1.call-update) | async-done | bytes 8388624 | tf_op jit(solution)/shard_map/all_gather | solution.py:35
  71.7 0.0 copy-done
  71.7 10.3 %fusion.29 = f32[256,2048]{1,0:T(8,128)S(1)} fusion(bf16[2048,2048]{1,0:T(8,128)(2,1)} %all-gather.9.cloned.1.call-done, bf16[1,2048,2048]{2,1,0:T(8,128)(2,1)} %param.8, bf16[1,256,2048]{2,1,0:T(8,128)(2,1)S(1)} %copy-done), kind=kOutput, calls=%fused_computation.20 | convolution fusion | flops 4295491584 | bytes 19922944 | tf_op jit(solution)/shard_map/cij,ckj->cik/dot_general | solution.py:36
  82.0 6.9 %multiply_convert_fusion = bf16[16,256,2048]{2,1,0:T(8,128)(2,1)} fusion(f32[256,2048]{1,0:T(8,128)S(1)} %fusion.29, f32[16]{0:T(128)S(1)} %select_reduce_fusion), kind=kLoop, calls=%fused_computation | loop fusion | flops 16777216 | bytes 18874432 | tf_op jit(solution)/shard_map/convert_element_type | solution.py:45
  88.9 0.0 reduce-scatter.4.cloned.1.call-update
  88.9 35.0 %all-gather.7.cloned.1.call-done = bf16[1,2048,2048]{2,1,0:T(8,128)(2,1)} async-done(((bf16[1,256,2048]{2,1,0:T(8,128)(2,1)}), bf16[1,2048,2048]{2,1,0:T(8,128)(2,1)}) %all-gather.7.cloned.1.call-update) | async-done | bytes 8388624 | tf_op jit(solution)/shard_map/all_gather | solution.py:21
  123.9 0.0 copy-done.2
  123.9 7.0 %fusion.4 = f32[256,2048]{1,0:T(8,128)} fusion(bf16[1,2048,2048]{2,1,0:T(8,128)(2,1)} %all-gather.7.cloned.1.call-done, bf16[1,256,2048]{2,1,0:T(8,128)(2,1)S(1)} %copy-done.2), kind=kOutput, calls=%fused_computation.5 | convolution fusion | flops 2147483648 | bytes 11534336 | tf_op jit(solution)/shard_map/cij,cjk->cik/dot_general | solution.py:25
  130.9 44.6 %all-gather.5.cloned.1.call-done = bf16[1,2048,2048]{2,1,0:T(8,128)(2,1)} async-done(((bf16[1,256,2048]{2,1,0:T(8,128)(2,1)}), bf16[1,2048,2048]{2,1,0:T(8,128)(2,1)}) %all-gather.5.cloned.1.call-update) | async-done | bytes 8388624 | tf_op jit(solution)/shard_map/all_gather | solution.py:22
  175.5 7.3 %fusion.20 = bf16[1,256,2048]{2,1,0:T(8,128)(2,1)} fusion(f32[256,2048]{1,0:T(8,128)} %fusion.4, bf16[1,2048,2048]{2,1,0:T(8,128)(2,1)} %all-gather.5.cloned.1.call-done, bf16[1,256,2048]{2,1,0:T(8,128)(2,1)S(1)} %copy-done), kind=kOutput, calls=%fused_computation.15 | convolution fusion | flops 2148532224 | bytes 12582912 | tf_op jit(solution)/shard_map/cij,cjk->cik/dot_general | solution.py:24
  182.8 106.6 %reduce-scatter.4.cloned.1.call-done = bf16[1,256,2048]{2,1,0:T(8,128)(2,1)} async-done(((bf16[16,256,2048]{2,1,0:T(8,128)(2,1)}), bf16[1,256,2048]{2,1,0:T(8,128)(2,1)}) %reduce-scatter.4.cloned.1.call-update) | async-done | bytes 1048592
  (7 shorter events, 0.0 us)
Async XLA Ops:
  7.2 64.5 %all-gather.9.cloned.1.call-start = ((), (), s32[]{:S(2)}) async-start(), calls=%async_computation.3 | async-start | bytes 9437184 | tf_op jit(solution)/shard_map/all_gather | solution.py:35
  11.1 7.1 %copy-start.1 = (bf16[1,256,2048]{2,1,0:T(8,128)(2,1)}, bf16[1,256,2048]{2,1,0:T(8,128)(2,1)S(1)}, u32[]{:S(2)}) copy-start(bf16[1,256,2048]{2,1,0:T(8,128)(2,1)S(1)} %get-tuple-element.2) | copy-start | bytes 3145732
  11.1 8.7 %copy-start.3 = (f32[1,8]{1,0:T(1,128)S(1)}, f32[1,8]{1,0:T(1,128)}, u32[]{:S(2)}) copy-start(f32[1,8]{1,0:T(1,128)} %param.11) | copy-start | bytes 100
  11.1 8.7 %copy-start.4 = (s32[1,8]{1,0:T(1,128)S(1)}, s32[1,8]{1,0:T(1,128)}, u32[]{:S(2)}) copy-start(s32[1,8]{1,0:T(1,128)} %param.10) | copy-start | bytes 100
  11.1 60.6 %copy-start = (bf16[1,256,2048]{2,1,0:T(8,128)(2,1)S(1)}, bf16[1,256,2048]{2,1,0:T(8,128)(2,1)}, u32[]{:S(2)}) copy-start(bf16[1,256,2048]{2,1,0:T(8,128)(2,1)} %get-tuple-element.3) | copy-start | bytes 3145732
  18.2 105.7 %all-gather.7.cloned.1.call-start = ((), (), s32[]{:S(2)}) async-start(), calls=%async_computation.2 | async-start | bytes 9437184 | tf_op jit(solution)/shard_map/all_gather | solution.py:21
  19.0 156.5 %all-gather.5.cloned.1.call-start = ((), (), s32[]{:S(2)}) async-start(), calls=%async_computation.1 | async-start | bytes 9437184 | tf_op jit(solution)/shard_map/all_gather | solution.py:22
  19.7 269.7 %reduce-scatter.4.cloned.1.call-start = ((), (), s32[]{:S(2)}) async-start(), calls=%async_computation.4 | async-start | bytes 17825792
  88.9 35.0 %copy-start.2 = (bf16[1,256,2048]{2,1,0:T(8,128)(2,1)S(1)}, bf16[1,256,2048]{2,1,0:T(8,128)(2,1)}, u32[]{:S(2)}) copy-start(bf16[1,256,2048]{2,1,0:T(8,128)(2,1)} %copy-done.1) | copy-start | bytes 3145732
Sparse Core Ops, SparseCore 0:
  18.3 53.3 all-gather.8
  74.0 49.8 all-gather.6
  125.6 49.8 all-gather.4
  179.3 110.0 reduce-scatter.3
where the time goes:
time: 296 us
  waiting for transfers between devices  239 us (81%)
  matrix products  31.7 us (11%)
  between operations  14.5 us (5%)
  other arithmetic  10.2 us (3%)
    unnamed x5, waiting for transfers between devices  108 us
    all_gather x1, waiting for transfers between devices, body(): omega_full = lax.all_gather(omega_cross, 'pair', axis=1, tiled=True)  51.8 us
    all_gather x1, waiting for transfers between devices, body(): lax.all_gather(omega_m, 'pair', axis=1, tiled=True)  44.6 us
    all_gather x1, waiting for transfers between devices, body(): lax.all_gather(eta_m, 'pair', axis=1, tiled=True)  35 us
    dot_general x1, matrix products, body(): jnp.einsum('cij,ckj->cik', eta_cross, omega_full, preferred_element_type=...  10.3 us
    dot_general x1, matrix products, body(): jnp.einsum('cij,cjk->cik', eta_m, full_omega, preferred_element_type=jnp....  7.29 us
    dot_general x1, matrix products, body(): jnp.einsum('cij,cjk->cik', omega_m, recouple, preferred_element_type=jnp....  7.1 us
    dot_general x1, matrix products, body(): jnp.einsum('cij,cjk->cik', omega_m, full_eta, preferred_element_type=jnp....  7.04 us
  transfers between devices with their start and end apart: 4, of which 4 were waited for; matrix products, arithmetic and copies ran while one was open for 11% of the time, Pallas kernels for 0%

commit v1 on v0

v1 whole, which is shorter than its diff:
```python
import functools

import jax
import jax.numpy as jnp
from jax import lax
from jax.experimental import pallas as pl
from jax.experimental.pallas import tpu as pltpu
from jax.sharding import PartitionSpec as P

MESH = pl.DeviceIdType.MESH
BF = jnp.bfloat16
F32 = jnp.float32
NN = (((1,), (0,)), ((), ()))
NT = (((1,), (1,)), ((), ()))
SIDE = 4
PIECES = 4
COPIES = 128


def dot(a, b, dims):
    return lax.dot_general(a, b, dims, preferred_element_type=F32)


def kernel(
    states_ref, map_ref, coef_ref, eta_hbm, omega_hbm, rec_hbm, pair_hbm, cross_hbm,
    om, eta_half, eta_left, om_left, eta_near, rec, e_ref, f_ref,
    gath, own_sum, sum_next, sum_prev, sum_two, merge, fin_a, fin_b,
    acc, pair_out, pair_send, cross_out, wrow, wvec,
    ssem, rsem, lsem,
):
    rows, width = eta_hbm.shape
    half = width // 2
    quarter = rows
    sub = rows // PIECES
    ch, pr = lax.axis_index("chan"), lax.axis_index("pair")
    y, z, x, c = ch // SIDE, ch % SIDE, pr // 2, pr % 2
    dn = 1 - 2 * ((x + c) % 2)
    xn, xf, xo = (x + dn + SIDE) % SIDE, (x - dn + SIDE) % SIDE, (x + 2) % SIDE
    turn = 1 - 2 * c
    h = x % 2
    hf = 1 - h
    near, far, sib = (ch, xn * 2 + c), (ch, xf * 2 + c), (ch, x * 2 + (1 - c))

    def along_y(d):
        return (((y + d + SIDE) % SIDE) * SIDE + z, pr)

    def along_z(d):
        return (y * SIDE + (z + d + SIDE) % SIDE, pr)

    moves = (along_z, along_y)
    live = states_ref[0]

    def at(ref, start, size, cols=None):
        start = pl.multiple_of(start, 16)
        if cols is None:
            return ref.at[pl.ds(start, size)]
        return ref.at[pl.ds(start, size), pl.ds(pl.multiple_of(cols[0], 128), cols[1])]

    count = [0, 0]

    def send(src, dst, device):
        i = count[0]
        count[0] += 1
        copy = pltpu.make_async_remote_copy(
            src_ref=src, dst_ref=dst, send_sem=ssem.at[i], recv_sem=rsem.at[i], device_id=device, device_id_type=MESH
        )
        copy.start()
        started.append(copy)
        return copy

    def local(src, dst):
        i = count[1]
        count[1] += 1
        copy = pltpu.make_async_copy(src, dst, lsem.at[i])
        copy.start()
        return copy

    started = []

    greeted = [near, far, sib, along_y(1), along_y(-1), along_y(2), along_z(1), along_z(-1), along_z(2)]
    barrier = pltpu.get_barrier_semaphore()
    for device in greeted:
        pl.semaphore_signal(barrier, inc=1, device_id=device, device_id_type=MESH)

    mine, theirs_n, theirs_f, theirs_o = pr * rows, (xn * 2 + c) * rows, (xf * 2 + c) * rows, (xo * 2 + c) * rows
    get_eta = local(eta_hbm, eta_left.at[pl.ds(0, rows)])
    tile = width // 4
    get_rec = [local(rec_hbm.at[:, pl.ds(t * tile, tile)], rec.at[:, pl.ds(t * tile, tile)]) for t in range(4)]
    get_om = local(omega_hbm, at(om, mine, rows))
    get_half = local(eta_hbm.at[:, pl.ds(pl.multiple_of(h * half, 128), half)], at(eta_half, mine, rows))

    pl.semaphore_wait(barrier, len(greeted))

    om_near, om_far = [], []
    for r in range(PIECES):
        src = omega_hbm.at[pl.ds(r * sub, sub)]
        dst = at(om, mine + r * sub, sub)
        om_near.append(send(src, dst, near))
        om_far.append(send(src, dst, far))
    om_sib = send(omega_hbm, at(om, mine, rows), sib)
    eh_sib = send(eta_hbm.at[:, pl.ds(pl.multiple_of(h * half, 128), half)], at(eta_half, mine, rows), sib)

    lane = lax.broadcasted_iota(jnp.int32, (8, 128), 1)
    weights = jnp.zeros((8, 128), F32)
    for f in range(map_ref.shape[1]):
        weights += jnp.where(lane == map_ref[0, f], coef_ref[0, f], 0.0)
    wrow[0] = weights
    got_w = []
    for m in range(2):
        for slot, d in ((1, 1), (2, -1), (3, 2)):
            got_w.append(send(wrow.at[0], wrow.at[1 + m * 3 + {1: 2, -1: 1, 2: 3}[d] - 1], moves[m](d)))

    row_no = lax.broadcasted_iota(jnp.int32, (rows, 1), 0)
    col_no = lax.broadcasted_iota(jnp.int32, (1, width), 1)

    def masked(block, first):
        keep = (row_no + first < live) & (col_no < live)
        return jnp.where(keep, block, jnp.zeros((), BF))

    get_eta.wait()
    eta_left[0:rows, :] = masked(eta_left[0:rows, :], mine)
    for t in range(4):
        get_rec[t].wait()
        e_ref[:, t * tile : (t + 1) * tile] = dot(eta_left[0:rows, :], rec[:, t * tile : (t + 1) * tile], NN).astype(BF)
    for t in range(4):
        part = dot(e_ref[...], rec[t * tile : (t + 1) * tile, :], NT)
        keep = lax.broadcasted_iota(jnp.int32, (1, tile), 1) + t * tile < live
        f_ref[:, t * tile : (t + 1) * tile] = jnp.where(keep, part, 0.0).astype(BF)

    om_on, om_near_sib, om_far_sib, om_opp_sib = [], [], [], []

    def pass_on(r):
        om_near[r].wait_recv()
        block = at(om, theirs_n + r * sub, sub)
        om_on.append(send(block, block, far))
        om_near_sib.append(send(block, block, sib))
        om_far[r].wait_recv()
        block = at(om, theirs_f + r * sub, sub)
        om_far_sib.append(send(block, block, sib))

    def pass_opposite(r):
        om_on[r].wait_recv()
        block = at(om, theirs_o + r * sub, sub)
        om_opp_sib.append(send(block, block, sib))

    chips = [x, (x + 1) % SIDE, (x + SIDE - 1) % SIDE, xo]
    quads = {}

    def product(p):
        first = pl.multiple_of(chips[p] * 2 * rows, 16)
        part = dot(f_ref[...], om[pl.ds(first, 2 * rows), :], NT)
        keep = lax.broadcasted_iota(jnp.int32, (1, 2 * rows), 1) + first < live
        part = jnp.where(keep, part, 0.0).astype(BF)
        for m in range(2):
            gath[m, p, 0] = part[:, m * rows : (m + 1) * rows]
            ahead = send(gath.at[m, p, 0], gath.at[m, p, 1], moves[m](turn))
            back = send(gath.at[m, p, 0], gath.at[m, p, 2], moves[m](-turn))
            quads[m, p] = [ahead, back]

    def gather_on(p):
        for m in range(2):
            quads[m, p][0].wait_recv()
            quads[m, p].append(send(gath.at[m, p, 1], gath.at[m, p, 3], moves[m](turn)))

    def weigh(p):
        for m in range(2):
            quads[m, p][1].wait_recv()
            quads[m, p][2].wait_recv()

            def step(i, carry, m=m):
                at_rows = pl.ds(pl.multiple_of(i * sub, 16), sub)
                parts = [gath[m, p, s, at_rows, :].astype(F32) for s in range(4)]
                for t, out in enumerate((own_sum, sum_next, sum_prev, sum_two)):
                    total = sum(wvec[m * 16 + t * 4 + s : m * 16 + t * 4 + s + 1, :] * parts[s] for s in range(4))
                    out[m, p, at_rows, :] = total.astype(out.dtype)
                return carry

            lax.fori_loop(0, PIECES, step, 0)
            other = moves[1 - m]
            two = send(sum_two.at[m, p], merge.at[m, p], other(turn))
            prev = send(sum_prev.at[m, p], fin_a.at[m, p], other(-turn))
            quads[m, p] += [two, prev]

    def merge_on(p):
        for m in range(2):
            quads[m, p][3].wait_recv()
            sum_next[m, p] = (sum_next[m, p].astype(F32) + merge[m, p].astype(F32)).astype(BF)
            quads[m, p].append(send(sum_next.at[m, p], fin_b.at[m, p], moves[1 - m](turn)))

    cross_done = []

    def finish(p):
        for m in range(2):
            quads[m, p][4].wait_recv()
            quads[m, p][5].wait_recv()
            total = own_sum[m, p] + fin_a[m, p].astype(F32) + fin_b[m, p].astype(F32)
            cross_out[m, p] = total.astype(BF)
            first = pl.multiple_of(chips[p] * 2 * rows + m * rows, 128)
            cross_done.append(local(cross_out.at[m, p], cross_hbm.at[:, pl.ds(first, rows)]))

    om_sib.wait_recv()
    get_om.wait()
    product(0)
    pass_on(0)

    for copy in got_w:
        copy.wait_recv()
    for m in range(2):
        for t, d in enumerate((0, turn, -turn, 2)):
            target = along_y(d)[0] if m == 0 else along_z(d)[0]
            for s in range(4):
                if s == 0:
                    row = wrow[0]
                elif s == 3:
                    row = wrow[1 + m * 3 + 2]
                else:
                    plus, minus = wrow[1 + m * 3], wrow[1 + m * 3 + 1]
                    row = jnp.where((turn if s == 2 else -turn) == 1, plus, minus)
                value = jnp.sum(jnp.where(lane == target, row, 0.0), axis=1, keepdims=True)[0:1]
                i = m * 16 + t * 4 + s
                wvec[i : i + 1, :] = jnp.broadcast_to(value, (1, wvec.shape[1]))

    om_left[0:rows, :] = masked(om[pl.ds(pl.multiple_of(mine, 16), rows), :], mine)
    gather_on(0)
    pass_on(1)
    weigh(0)
    pass_on(2)
    merge_on(0)
    pass_on(3)

    eta_n = []

    def eta_to_near(r):
        eta_n.append(send(eta_hbm.at[pl.ds(r * sub, sub)], eta_near.at[pl.ds(r * sub, sub)], near))

    def eta_cols(q, side):
        return pl.ds(pl.multiple_of(side * half + q * quarter, 128), quarter)

    eta_to_near(0)
    for r in range(PIECES):
        om_near_sib[r].wait_recv()
        om_far_sib[r].wait_recv()
    product(1)
    product(2)
    finish(0)
    pass_opposite(0)
    gather_on(1)
    eta_to_near(1)
    pass_opposite(1)
    gather_on(2)
    eta_to_near(2)
    om_left[rows:, :] = masked(om[pl.ds(pl.multiple_of(theirs_n, 16), rows), :], theirs_n)
    weigh(1)
    pass_opposite(2)
    eta_to_near(3)
    weigh(2)
    pass_opposite(3)

    eta_f, eta_on, eta_n_sib, eta_f_sib, eta_o_sib = [], [], [], [], []

    def eta_to_far(q):
        eta_f.append(send(eta_hbm.at[:, eta_cols(q, hf)], at(eta_half, mine, rows, (q * quarter, quarter)), far))

    def eta_pass(q):
        eta_on.append(send(eta_near.at[:, eta_cols(q, hf)], at(eta_half, theirs_n, rows, (q * quarter, quarter)), far))

    eta_to_far(0)
    for r in range(PIECES):
        om_opp_sib[r].wait_recv()
    product(3)
    merge_on(1)
    merge_on(2)
    gather_on(3)

    half_cols = pl.ds(pl.multiple_of(h * half, 128), half)

    def first_term(lo):
        for t in range(half // 512):
            cols = pl.ds(pl.multiple_of(h * half + t * 512, 128), 512)
            acc[lo : lo + rows, t * 512 : (t + 1) * 512] = dot(eta_left[lo : lo + rows, :], om[:, cols], NN)

    first_term(0)
    eta_to_far(1)
    weigh(3)

    for r in range(PIECES):
        eta_n[r].wait_recv()
    eta_pass(0)
    eta_pass(1)
    eta_to_far(2)
    eta_pass(2)
    eta_to_far(3)
    eta_pass(3)
    eta_n_sib = send(eta_near.at[:, half_cols], at(eta_half, theirs_n, rows), sib)
    own_copy = local(eta_near.at[:, half_cols], at(eta_half, theirs_n, rows))
    eta_left[rows:, :] = masked(eta_near[...], theirs_n)
    finish(1)
    finish(2)
    first_term(rows)
    merge_on(3)
    get_half.wait()
    eh_sib.wait_recv()
    eta_n_sib.wait_recv()
    own_copy.wait()

    swaps, pair_done = [], []
    for q in range(PIECES):
        eta_f[q].wait_recv()
        block = at(eta_half, theirs_f, rows, (q * quarter, quarter))
        eta_f_sib.append(send(block, block, sib))
        eta_on[q].wait_recv()
        block = at(eta_half, theirs_o, rows, (q * quarter, quarter))
        eta_o_sib.append(send(block, block, sib))
        if q == 1:
            finish(3)
        eta_f_sib[q].wait_recv()
        eta_o_sib[q].wait_recv()
        cols = slice(q * quarter, (q + 1) * quarter)
        part = acc[:, cols] - dot(om_left[...], eta_half[:, cols], NN)
        keep = lax.broadcasted_iota(jnp.int32, (1, quarter), 1) + h * half + q * quarter < live
        part = jnp.where(keep, part, 0.0).astype(BF)
        pair_send[q] = part[rows:]
        swaps.append(send(pair_send.at[q], pair_out.at[1, q], near))
        pair_out[0, q] = part[:rows]
        pair_done.append(local(pair_out.at[0, q], pair_hbm.at[:, eta_cols(q, h)]))
    for q in range(PIECES):
        swaps[q].wait_recv()
        pair_done.append(local(pair_out.at[1, q], pair_hbm.at[:, eta_cols(q, hf)]))
    for copy in started:
        copy.wait_send()
    for copy in pair_done + cross_done:
        copy.wait()


def body(eta_blocks, omega_blocks, recouple, block_states, cross_map, cross_coef):
    rows, width = eta_blocks.shape[1:]
    half = width // 2
    any_space = pl.BlockSpec(memory_space=pl.ANY)
    smem = pl.BlockSpec(memory_space=pltpu.SMEM)
    square = (2, SIDE, rows, rows)
    out = jax.ShapeDtypeStruct((rows, width), BF)
    pair_comm, cross_comm = pl.pallas_call(
        kernel,
        out_shape=(out, out),
        in_specs=[smem] * 3 + [any_space] * 3,
        out_specs=(any_space, any_space),
        scratch_shapes=[
            pltpu.VMEM((width, width), BF),
            pltpu.VMEM((width, half), BF),
            pltpu.VMEM((2 * rows, width), BF),
            pltpu.VMEM((2 * rows, width), BF),
            pltpu.VMEM((rows, width), BF),
            pltpu.VMEM((width, width), BF),
            pltpu.VMEM((rows, width), BF),
            pltpu.VMEM((rows, width), BF),
            pltpu.VMEM((2, SIDE, SIDE, rows, rows), BF),
            pltpu.VMEM(square, F32),
            pltpu.VMEM(square, BF),
            pltpu.VMEM(square, BF),
            pltpu.VMEM(square, BF),
            pltpu.VMEM(square, BF),
            pltpu.VMEM(square, BF),
            pltpu.VMEM(square, BF),
            pltpu.VMEM((2 * rows, half), F32),
            pltpu.VMEM(square, BF),
            pltpu.VMEM((SIDE, rows, rows), BF),
            pltpu.VMEM(square, BF),
            pltpu.VMEM((7, 8, 128), F32),
            pltpu.VMEM((32, rows), F32),
            pltpu.SemaphoreType.DMA((COPIES,)),
            pltpu.SemaphoreType.DMA((COPIES,)),
            pltpu.SemaphoreType.DMA((32,)),
        ],
        compiler_params=pltpu.CompilerParams(collective_id=0, has_side_effects=True, vmem_limit_bytes=60 * 1024 * 1024),
        cost_estimate=pl.CostEstimate(flops=10 * rows * width * width, bytes_accessed=14 * rows * width * 2, transcendentals=0),
        name="commutators",
    )(block_states, cross_map, cross_coef, eta_blocks[0], omega_blocks[0], recouple[0])
    return pair_comm[None], cross_comm[None]


def solution(mesh):
    placed = (
        P("chan", "pair", None),
        P("chan", "pair", None),
        P("chan", None, None),
        P("chan"),
        P("chan", None),
        P("chan", None),
    )
    return jax.shard_map(
        body,
        mesh=mesh,
        in_specs=placed,
        out_specs=(P("chan", "pair", None), P("chan", "pair", None)),
        check_vma=False,
    )
```

time: 296 us -> 92.3 us (0.31)
  waiting for transfers between devices: 239 us -> 0 us
  Pallas kernels: 0 us -> 86.2 us
  matrix products: 31.7 us -> 0 us
  between operations: 14.5 us -> 1.29 us
  other arithmetic: 10.2 us -> 0 us
  local copies, waits for them, and re-layouts: 0.02 us -> 4.61 us
    all_gather x3 -> x0, waiting for transfers between devices: 131 us -> none  [the longest x1 51.8 us: body(): omega_full = lax.all_gather(omega_cross, 'pair', axis=1, tiled=True)]
    unnamed x5 -> x0, waiting for transfers between devices: 108 us -> none
    pallas_call x0 -> x1, Pallas kernels: none -> 86.2 us  [body(): pl.pallas_call(kernel, out_shape=(out, out), in_specs=[smem] * 3 + [any_s...]
    dot_general x4 -> x0, matrix products: 31.7 us -> none  [the longest x1 10.3 us: body(): jnp.einsum('cij,ckj->cik', eta_cross, omega_full, preferred_element_type=...]
    convert_element_type x1 -> x0, other arithmetic: 6.9 us -> none  [body(): summed.astype(jnp.bfloat16)]
    unnamed x10 -> x2, local copies, waits for them, and re-layouts: 0.02 us -> 4.61 us
    select_n x1 -> x0, other arithmetic: 3.17 us -> none  [body(): omega_m = jnp.where(live, omega_blocks, zero_bf)]
  transfers between devices with their start and end apart: 4 -> 0, of which waited for: 4 -> 0; matrix products, arithmetic and copies ran while one was open for 11% -> 0% of each run, Pallas kernels for 0% -> 0%
where the time goes in v1:
time: 92.3 us; the launch traced here: 92.1 us
  Pallas kernels  86.2 us (93%)
  local copies, waits for them, and re-layouts  4.61 us (5%)
  between operations  1.29 us (1%)
    pallas_call x1, Pallas kernels, body(): pl.pallas_call(kernel, out_shape=(out, out), in_specs=[smem] * 3 + [any_s...  86.2 us
    unnamed x2, local copies, waits for them, and re-layouts  4.61 us

profile of v1, /device:TPU:1, one launch (start us, length us, event | category | flops | bytes accessed | tf_op | source)
XLA Modules:
  0.0 92.1 jit_solution(13594569285792695405)
XLA Ops:
  1.3 86.2 %commutators.1 = (bf16[256,2048]{1,0:T(8,128)(2,1)}, bf16[256,2048]{1,0:T(8,128)(2,1)}) custom-call(s32[1]{0:T(128)S(6)} %copy.10.states_ref, s32[1,8]{1,0:T(1,128)} %map_ref.1, f32[1,8]{1,0:T(1,128)} %coef_ref.1, bf16[256,2048]{1,0:T(8,128)(2,1)} %bitcast.8, bf16[256,2048]{1,0:T(8,128)(2,1)} %bitcast.9, bf16[2048,2048]{1,0:T(8,128)(2,1)} %bitcast.7), custom_call_target="tpu_custom_call" | custom-call | flops 10737418240 | bytes 14680064 | tf_op jit(solution)/shard_map/commutators/pallas_call | solution.py:342
  87.5 2.3 %copy.11 = bf16[1,256,2048]{2,1,0:T(8,128)(2,1)} copy(bf16[1,256,2048]{2,1,0:T(8,128)(2,1)} %bitcast.6) | data formatting | bytes 2097152
  89.8 2.3 %copy.12 = bf16[1,256,2048]{2,1,0:T(8,128)(2,1)} copy(bf16[1,256,2048]{2,1,0:T(8,128)(2,1)} %bitcast.5) | data formatting | bytes 2097152

commit v2 on v1

--- a/solution.py
+++ b/solution.py
@@ -22,10 +22,10 @@
 
 
 def kernel(
-    states_ref, map_ref, coef_ref, eta_hbm, omega_hbm, rec_hbm, pair_hbm, cross_hbm,
+    states_ref, map_ref, coef_ref, eta_hbm, omega_hbm, rec_hbm, pair_ref, cross_ref,
     om, eta_half, eta_left, om_left, eta_near, rec, e_ref, f_ref,
     gath, own_sum, sum_next, sum_prev, sum_two, merge, fin_a, fin_b,
-    acc, pair_out, pair_send, cross_out, wrow, wvec,
+    acc, pair_send, wrow, wvec,
     ssem, rsem, lsem,
 ):
     rows, width = eta_hbm.shape
@@ -91,12 +91,13 @@
 
     pl.semaphore_wait(barrier, len(greeted))
 
-    om_near, om_far = [], []
+    om_near, om_far = {}, {}
+
+    def omega_to(r, device, kept):
+        kept[r] = send(omega_hbm.at[pl.ds(r * sub, sub)], at(om, mine + r * sub, sub), device)
+
     for r in range(PIECES):
-        src = omega_hbm.at[pl.ds(r * sub, sub)]
-        dst = at(om, mine + r * sub, sub)
-        om_near.append(send(src, dst, near))
-        om_far.append(send(src, dst, far))
+        omega_to(r, near, om_near)
     om_sib = send(omega_hbm, at(om, mine, rows), sib)
     eh_sib = send(eta_hbm.at[:, pl.ds(pl.multiple_of(h * half, 128), half)], at(eta_half, mine, rows), sib)
 
@@ -117,42 +118,44 @@
         keep = (row_no + first < live) & (col_no < live)
         return jnp.where(keep, block, jnp.zeros((), BF))
 
-    get_eta.wait()
-    eta_left[0:rows, :] = masked(eta_left[0:rows, :], mine)
-    for t in range(4):
-        get_rec[t].wait()
-        e_ref[:, t * tile : (t + 1) * tile] = dot(eta_left[0:rows, :], rec[:, t * tile : (t + 1) * tile], NN).astype(BF)
-    for t in range(4):
-        part = dot(e_ref[...], rec[t * tile : (t + 1) * tile, :], NT)
-        keep = lax.broadcasted_iota(jnp.int32, (1, tile), 1) + t * tile < live
-        f_ref[:, t * tile : (t + 1) * tile] = jnp.where(keep, part, 0.0).astype(BF)
-
-    om_on, om_near_sib, om_far_sib, om_opp_sib = [], [], [], []
-
-    def pass_on(r):
+    om_on, om_near_sib, om_far_sib, om_opp_sib = {}, {}, {}, {}
+
+    def near_omega(r):
         om_near[r].wait_recv()
         block = at(om, theirs_n + r * sub, sub)
-        om_on.append(send(block, block, far))
-        om_near_sib.append(send(block, block, sib))
+        om_near_sib[r] = send(block, block, sib)
+
+    def omega_to_far(r):
+        omega_to(r, far, om_far)
+
+    def far_omega(r):
         om_far[r].wait_recv()
         block = at(om, theirs_f + r * sub, sub)
-        om_far_sib.append(send(block, block, sib))
-
-    def pass_opposite(r):
+        om_far_sib[r] = send(block, block, sib)
+
+    def pass_omega(r):
+        block = at(om, theirs_n + r * sub, sub)
+        om_on[r] = send(block, block, far)
+
+    def opposite_omega(r):
         om_on[r].wait_recv()
         block = at(om, theirs_o + r * sub, sub)
-        om_opp_sib.append(send(block, block, sib))
-
-    chips = [x, (x + 1) % SIDE, (x + SIDE - 1) % SIDE, xo]
+        om_opp_sib[r] = send(block, block, sib)
+
+    def from_sibling(copies):
+        for r in range(PIECES):
+            copies[r].wait_recv()
+
+    step0 = 1 - 2 * (x % 2)
+    chips = [(x, x), ((x + step0 + SIDE) % SIDE, (x - step0 + SIDE) % SIDE), ((x - step0 + SIDE) % SIDE, (x + step0 + SIDE) % SIDE), (xo, xo)]
     quads = {}
 
     def product(p):
-        first = pl.multiple_of(chips[p] * 2 * rows, 16)
-        part = dot(f_ref[...], om[pl.ds(first, 2 * rows), :], NT)
-        keep = lax.broadcasted_iota(jnp.int32, (1, 2 * rows), 1) + first < live
-        part = jnp.where(keep, part, 0.0).astype(BF)
-        for m in range(2):
-            gath[m, p, 0] = part[:, m * rows : (m + 1) * rows]
+        for m in range(2):
+            first = pl.multiple_of((chips[p][m] * 2 + m) * rows, 128)
+            part = dot(f_ref[...], om[pl.ds(first, rows), :], NT)
+            keep = lax.broadcasted_iota(jnp.int32, (1, rows), 1) + first < live
+            gath[m, p, 0] = jnp.where(keep, part, 0.0).astype(BF)
             ahead = send(gath.at[m, p, 0], gath.at[m, p, 1], moves[m](turn))
             back = send(gath.at[m, p, 0], gath.at[m, p, 2], moves[m](-turn))
             quads[m, p] = [ahead, back]
@@ -187,90 +190,68 @@
             sum_next[m, p] = (sum_next[m, p].astype(F32) + merge[m, p].astype(F32)).astype(BF)
             quads[m, p].append(send(sum_next.at[m, p], fin_b.at[m, p], moves[1 - m](turn)))
 
-    cross_done = []
-
     def finish(p):
         for m in range(2):
             quads[m, p][4].wait_recv()
             quads[m, p][5].wait_recv()
             total = own_sum[m, p] + fin_a[m, p].astype(F32) + fin_b[m, p].astype(F32)
-            cross_out[m, p] = total.astype(BF)
-            first = pl.multiple_of(chips[p] * 2 * rows + m * rows, 128)
-            cross_done.append(local(cross_out.at[m, p], cross_hbm.at[:, pl.ds(first, rows)]))
-
-    om_sib.wait_recv()
-    get_om.wait()
-    product(0)
-    pass_on(0)
-
-    for copy in got_w:
-        copy.wait_recv()
-    for m in range(2):
-        for t, d in enumerate((0, turn, -turn, 2)):
-            target = along_y(d)[0] if m == 0 else along_z(d)[0]
-            for s in range(4):
-                if s == 0:
-                    row = wrow[0]
-                elif s == 3:
-                    row = wrow[1 + m * 3 + 2]
-                else:
-                    plus, minus = wrow[1 + m * 3], wrow[1 + m * 3 + 1]
-                    row = jnp.where((turn if s == 2 else -turn) == 1, plus, minus)
-                value = jnp.sum(jnp.where(lane == target, row, 0.0), axis=1, keepdims=True)[0:1]
-                i = m * 16 + t * 4 + s
-                wvec[i : i + 1, :] = jnp.broadcast_to(value, (1, wvec.shape[1]))
-
-    om_left[0:rows, :] = masked(om[pl.ds(pl.multiple_of(mine, 16), rows), :], mine)
-    gather_on(0)
-    pass_on(1)
-    weigh(0)
-    pass_on(2)
-    merge_on(0)
-    pass_on(3)
-
-    eta_n = []
+            first = pl.multiple_of((chips[p][m] * 2 + m) * rows, 128)
+            cross_ref[:, pl.ds(first, rows)] = total.astype(BF)
+
+    def recouple():
+        get_eta.wait()
+        eta_left[0:rows, :] = masked(eta_left[0:rows, :], mine)
+        for t in range(4):
+            get_rec[t].wait()
+            e_ref[:, t * tile : (t + 1) * tile] = dot(eta_left[0:rows, :], rec[:, t * tile : (t + 1) * tile], NN).astype(BF)
+
+    def recouple_back():
+        for t in range(4):
+            part = dot(e_ref[...], rec[t * tile : (t + 1) * tile, :], NT)
+            keep = lax.broadcasted_iota(jnp.int32, (1, tile), 1) + t * tile < live
+            f_ref[:, t * tile : (t + 1) * tile] = jnp.where(keep, part, 0.0).astype(BF)
+
+    def own_omega():
+        om_sib.wait_recv()
+        get_om.wait()
+
+    def set_weights():
+        for copy in got_w:
+            copy.wait_recv()
+        for m in range(2):
+            for t, d in enumerate((0, turn, -turn, 2)):
+                target = along_y(d)[0] if m == 0 else along_z(d)[0]
+                for s in range(4):
+                    if s == 0:
+                        row = wrow[0]
+                    elif s == 3:
+                        row = wrow[1 + m * 3 + 2]
+                    else:
+                        plus, minus = wrow[1 + m * 3], wrow[1 + m * 3 + 1]
+                        row = jnp.where((turn if s == 2 else -turn) == 1, plus, minus)
+                    value = jnp.sum(jnp.where(lane == target, row, 0.0), axis=1, keepdims=True)[0:1]
+                    i = m * 16 + t * 4 + s
+                    wvec[i : i + 1, :] = jnp.broadcast_to(value, (1, wvec.shape[1]))
+
+    def own_left():
+        om_left[0:rows, :] = masked(om[pl.ds(pl.multiple_of(mine, 16), rows), :], mine)
+
+    def near_left():
+        om_left[rows:, :] = masked(om[pl.ds(pl.multiple_of(theirs_n, 16), rows), :], theirs_n)
+
+    eta_n, eta_f, eta_on, eta_f_sib, eta_o_sib, eta_n_sib, own_copy = {}, {}, {}, {}, {}, [], []
 
     def eta_to_near(r):
-        eta_n.append(send(eta_hbm.at[pl.ds(r * sub, sub)], eta_near.at[pl.ds(r * sub, sub)], near))
+        eta_n[r] = send(eta_hbm.at[pl.ds(r * sub, sub)], eta_near.at[pl.ds(r * sub, sub)], near)
 
     def eta_cols(q, side):
         return pl.ds(pl.multiple_of(side * half + q * quarter, 128), quarter)
 
-    eta_to_near(0)
-    for r in range(PIECES):
-        om_near_sib[r].wait_recv()
-        om_far_sib[r].wait_recv()
-    product(1)
-    product(2)
-    finish(0)
-    pass_opposite(0)
-    gather_on(1)
-    eta_to_near(1)
-    pass_opposite(1)
-    gather_on(2)
-    eta_to_near(2)
-    om_left[rows:, :] = masked(om[pl.ds(pl.multiple_of(theirs_n, 16), rows), :], theirs_n)
-    weigh(1)
-    pass_opposite(2)
-    eta_to_near(3)
-    weigh(2)
-    pass_opposite(3)
-
-    eta_f, eta_on, eta_n_sib, eta_f_sib, eta_o_sib = [], [], [], [], []
-
     def eta_to_far(q):
-        eta_f.append(send(eta_hbm.at[:, eta_cols(q, hf)], at(eta_half, mine, rows, (q * quarter, quarter)), far))
+        eta_f[q] = send(eta_hbm.at[:, eta_cols(q, hf)], at(eta_half, mine, rows, (q * quarter, quarter)), far)
 
     def eta_pass(q):
-        eta_on.append(send(eta_near.at[:, eta_cols(q, hf)], at(eta_half, theirs_n, rows, (q * quarter, quarter)), far))
-
-    eta_to_far(0)
-    for r in range(PIECES):
-        om_opp_sib[r].wait_recv()
-    product(3)
-    merge_on(1)
-    merge_on(2)
-    gather_on(3)
+        eta_on[q] = send(eta_near.at[:, eta_cols(q, hf)], at(eta_half, theirs_n, rows, (q * quarter, quarter)), far)
 
     half_cols = pl.ds(pl.multiple_of(h * half, 128), half)
 
@@ -279,40 +260,32 @@
             cols = pl.ds(pl.multiple_of(h * half + t * 512, 128), 512)
             acc[lo : lo + rows, t * 512 : (t + 1) * 512] = dot(eta_left[lo : lo + rows, :], om[:, cols], NN)
 
-    first_term(0)
-    eta_to_far(1)
-    weigh(3)
-
-    for r in range(PIECES):
-        eta_n[r].wait_recv()
-    eta_pass(0)
-    eta_pass(1)
-    eta_to_far(2)
-    eta_pass(2)
-    eta_to_far(3)
-    eta_pass(3)
-    eta_n_sib = send(eta_near.at[:, half_cols], at(eta_half, theirs_n, rows), sib)
-    own_copy = local(eta_near.at[:, half_cols], at(eta_half, theirs_n, rows))
-    eta_left[rows:, :] = masked(eta_near[...], theirs_n)
-    finish(1)
-    finish(2)
-    first_term(rows)
-    merge_on(3)
-    get_half.wait()
-    eh_sib.wait_recv()
-    eta_n_sib.wait_recv()
-    own_copy.wait()
-
-    swaps, pair_done = [], []
-    for q in range(PIECES):
+    def near_eta():
+        for r in range(PIECES):
+            eta_n[r].wait_recv()
+
+    def share_near_eta():
+        eta_n_sib.append(send(eta_near.at[:, half_cols], at(eta_half, theirs_n, rows), sib))
+        own_copy.append(local(eta_near.at[:, half_cols], at(eta_half, theirs_n, rows)))
+        eta_left[rows:, :] = masked(eta_near[...], theirs_n)
+
+    def settle_eta():
+        get_half.wait()
+        eh_sib.wait_recv()
+        eta_n_sib[0].wait_recv()
+        own_copy[0].wait()
+
+    swaps = {}
+
+    def share_eta(q):
         eta_f[q].wait_recv()
         block = at(eta_half, theirs_f, rows, (q * quarter, quarter))
-        eta_f_sib.append(send(block, block, sib))
+        eta_f_sib[q] = send(block, block, sib)
         eta_on[q].wait_recv()
         block = at(eta_half, theirs_o, rows, (q * quarter, quarter))
-        eta_o_sib.append(send(block, block, sib))
-        if q == 1:
-            finish(3)
+        eta_o_sib[q] = send(block, block, sib)
+
+    def last_term(q):
         eta_f_sib[q].wait_recv()
         eta_o_sib[q].wait_recv()
         cols = slice(q * quarter, (q + 1) * quarter)
@@ -320,16 +293,28 @@
         keep = lax.broadcasted_iota(jnp.int32, (1, quarter), 1) + h * half + q * quarter < live
         part = jnp.where(keep, part, 0.0).astype(BF)
         pair_send[q] = part[rows:]
-        swaps.append(send(pair_send.at[q], pair_out.at[1, q], near))
-        pair_out[0, q] = part[:rows]
-        pair_done.append(local(pair_out.at[0, q], pair_hbm.at[:, eta_cols(q, h)]))
-    for q in range(PIECES):
+        swaps[q] = send(pair_send.at[q], pair_ref.at[:, eta_cols(q, h)], near)
+        pair_ref[:, eta_cols(q, h)] = part[:rows]
+
+    def swapped(q):
         swaps[q].wait_recv()
-        pair_done.append(local(pair_out.at[1, q], pair_hbm.at[:, eta_cols(q, hf)]))
+
+    plan = [
+        (omega_to_far, 0), (omega_to_far, 3), (recouple,), (own_omega,), (recouple_back,), (omega_to_far, 2), (omega_to_far, 1), (product, 0),
+        (near_omega, 1), (near_omega, 0), (pass_omega, 1), (near_omega, 3), (set_weights,), (eta_to_near, 3), (pass_omega, 3), (near_omega, 2),
+        (pass_omega, 0), (far_omega, 2), (far_omega, 0), (far_omega, 3), (from_sibling, om_near_sib), (gather_on, 0), (pass_omega, 2), (product, 1),
+        (eta_to_near, 0), (far_omega, 1), (eta_to_far, 0), (gather_on, 1), (near_left,), (weigh, 0), (from_sibling, om_far_sib), (product, 2),
+        (merge_on, 0), (weigh, 1), (eta_to_near, 2), (opposite_omega, 3), (gather_on, 2), (eta_to_near, 1), (opposite_omega, 1), (opposite_omega, 2),
+        (opposite_omega, 0), (from_sibling, om_opp_sib), (product, 3), (eta_to_far, 1), (near_eta,), (eta_pass, 1), (eta_pass, 0), (share_near_eta,),
+        (merge_on, 1), (first_term, rows), (gather_on, 3), (eta_to_far, 3), (weigh, 2), (eta_pass, 3), (first_term, 0), (share_eta, 1),
+        (eta_to_far, 2), (eta_pass, 2), (own_left,), (settle_eta,), (share_eta, 0), (finish, 0), (weigh, 3), (last_term, 0), (share_eta, 3),
+        (last_term, 1), (merge_on, 2), (share_eta, 2), (finish, 1), (last_term, 3), (merge_on, 3), (last_term, 2), (finish, 2), (finish, 3),
+        (swapped, 2), (swapped, 1), (swapped, 3), (swapped, 0),
+    ]
+    for step, *which in plan:
+        step(*which)
     for copy in started:
         copy.wait_send()
-    for copy in pair_done + cross_done:
-        copy.wait()
 
 
 def body(eta_blocks, omega_blocks, recouple, block_states, cross_map, cross_coef):
@@ -338,12 +323,12 @@
     any_space = pl.BlockSpec(memory_space=pl.ANY)
     smem = pl.BlockSpec(memory_space=pltpu.SMEM)
     square = (2, SIDE, rows, rows)
-    out = jax.ShapeDtypeStruct((rows, width), BF)
+    out = pltpu.VMEM((rows, width), BF)
     pair_comm, cross_comm = pl.pallas_call(
         kernel,
         out_shape=(out, out),
         in_specs=[smem] * 3 + [any_space] * 3,
-        out_specs=(any_space, any_space),
+        out_specs=(pl.BlockSpec(memory_space=pltpu.VMEM),) * 2,
         scratch_shapes=[
             pltpu.VMEM((width, width), BF),
             pltpu.VMEM((width, half), BF),
@@ -362,9 +347,7 @@
             pltpu.VMEM(square, BF),
             pltpu.VMEM(square, BF),
             pltpu.VMEM((2 * rows, half), F32),
-            pltpu.VMEM(square, BF),
             pltpu.VMEM((SIDE, rows, rows), BF),
-            pltpu.VMEM(square, BF),
             pltpu.VMEM((7, 8, 128), F32),
             pltpu.VMEM((32, rows), F32),
             pltpu.SemaphoreType.DMA((COPIES,)),

time: 92.3 us -> 86.6 us (0.938)
  Pallas kernels: 86.2 us -> 83.3 us
  local copies, waits for them, and re-layouts: 4.61 us -> 1.94 us
    pallas_call x1, Pallas kernels: 86.2 us -> 83.3 us  [body(): pl.pallas_call(kernel, out_shape=(out, out), in_specs=[smem] * 3 + [any_s...]
    unnamed x2, local copies, waits for them, and re-layouts: 4.61 us -> 1.94 us
where the time goes in v2:
time: 86.6 us; the launch traced here: 86.5 us
  Pallas kernels  83.3 us (96%)
  local copies, waits for them, and re-layouts  1.94 us (2%)
  between operations  1.29 us (1%)
    pallas_call x1, Pallas kernels, body(): pl.pallas_call(kernel, out_shape=(out, out), in_specs=[smem] * 3 + [any_s...  83.3 us
    unnamed x2, local copies, waits for them, and re-layouts  1.94 us

profile of v2, /device:TPU:1, one launch (start us, length us, event | category | flops | bytes accessed | tf_op | source)
XLA Modules:
  0.0 86.5 jit_solution(12855927138441327329)
XLA Ops:
  1.3 83.3 %commutators.1 = (bf16[256,2048]{1,0:T(8,128)(2,1)S(1)}, bf16[256,2048]{1,0:T(8,128)(2,1)S(1)}) custom-call(s32[1]{0:T(128)S(6)} %copy.12.states_ref, s32[1,8]{1,0:T(1,128)} %map_ref.1, f32[1,8]{1,0:T(1,128)} %coef_ref.1, bf16[256,2048]{1,0:T(8,128)(2,1)} %bitcast.8, bf16[256,2048]{1,0:T(8,128)(2,1)} %bitcast.9, bf16[2048,2048]{1,0:T(8,128)(2,1)} %bitcast.7), custom_call_target="tpu_custom_call" | custom-call | flops 10737418240 | bytes 14680064 | tf_op jit(solution)/shard_map/commutators/pallas_call | solution.py:327
  84.6 1.0 %copy.10 = bf16[1,256,2048]{2,1,0:T(8,128)(2,1)} copy(bf16[1,256,2048]{2,1,0:T(8,128)(2,1)S(1)} %bitcast.6) | data formatting | bytes 2097152
  85.5 1.0 %copy.11 = bf16[1,256,2048]{2,1,0:T(8,128)(2,1)} copy(bf16[1,256,2048]{2,1,0:T(8,128)(2,1)S(1)} %bitcast.5) | data formatting | bytes 2097152

commit v3 on v2

--- a/solution.py
+++ b/solution.py
@@ -26,7 +26,7 @@
     om, eta_half, eta_left, om_left, eta_near, rec, e_ref, f_ref,
     gath, own_sum, sum_next, sum_prev, sum_two, merge, fin_a, fin_b,
     acc, pair_send, wrow, wvec,
-    ssem, rsem, lsem,
+    ssem, rsem, lsem, answer, told,
 ):
     rows, width = eta_hbm.shape
     half = width // 2
@@ -77,10 +77,18 @@
 
     started = []
 
-    greeted = [near, far, sib, along_y(1), along_y(-1), along_y(2), along_z(1), along_z(-1), along_z(2)]
     barrier = pltpu.get_barrier_semaphore()
-    for device in greeted:
-        pl.semaphore_signal(barrier, inc=1, device_id=device, device_id_type=MESH)
+    even = (x + c) % 2 == 0
+    beside = (near, far, sib)
+    across = [move(d) for move in moves for d in (1, -1, 2)]
+
+    def signal(semaphore, device):
+        pl.semaphore_signal(semaphore, inc=1, device_id=device, device_id_type=MESH)
+
+    @pl.when(even)
+    def _():
+        for device in beside:
+            signal(barrier, device)
 
     mine, theirs_n, theirs_f, theirs_o = pr * rows, (xn * 2 + c) * rows, (xf * 2 + c) * rows, (xo * 2 + c) * rows
     get_eta = local(eta_hbm, eta_left.at[pl.ds(0, rows)])
@@ -89,7 +97,15 @@
     get_om = local(omega_hbm, at(om, mine, rows))
     get_half = local(eta_hbm.at[:, pl.ds(pl.multiple_of(h * half, 128), half)], at(eta_half, mine, rows))
 
-    pl.semaphore_wait(barrier, len(greeted))
+    @pl.when(jnp.logical_not(even))
+    def _():
+        pl.semaphore_wait(barrier, len(beside))
+        for device in beside:
+            signal(answer, device)
+
+    @pl.when(even)
+    def _():
+        pl.semaphore_wait(answer, len(beside))
 
     om_near, om_far = {}, {}
 
@@ -106,10 +122,26 @@
     for f in range(map_ref.shape[1]):
         weights += jnp.where(lane == map_ref[0, f], coef_ref[0, f], 0.0)
     wrow[0] = weights
+    @pl.when(even)
+    def _():
+        for device in across:
+            signal(barrier, device)
+
     got_w = []
-    for m in range(2):
-        for slot, d in ((1, 1), (2, -1), (3, 2)):
-            got_w.append(send(wrow.at[0], wrow.at[1 + m * 3 + {1: 2, -1: 1, 2: 3}[d] - 1], moves[m](d)))
+
+    def meet():
+        @pl.when(even)
+        def _():
+            pl.semaphore_wait(barrier, len(across))
+            signal(told, sib)
+
+        @pl.when(jnp.logical_not(even))
+        def _():
+            pl.semaphore_wait(told, 1)
+
+        for m in range(2):
+            for slot, d in ((1, 1), (2, -1), (3, 2)):
+                got_w.append(send(wrow.at[0], wrow.at[1 + m * 3 + {1: 2, -1: 1, 2: 3}[d] - 1], moves[m](d)))
 
     row_no = lax.broadcasted_iota(jnp.int32, (rows, 1), 0)
     col_no = lax.broadcasted_iota(jnp.int32, (1, width), 1)
@@ -300,16 +332,16 @@
         swaps[q].wait_recv()
 
     plan = [
-        (omega_to_far, 0), (omega_to_far, 3), (recouple,), (own_omega,), (recouple_back,), (omega_to_far, 2), (omega_to_far, 1), (product, 0),
-        (near_omega, 1), (near_omega, 0), (pass_omega, 1), (near_omega, 3), (set_weights,), (eta_to_near, 3), (pass_omega, 3), (near_omega, 2),
-        (pass_omega, 0), (far_omega, 2), (far_omega, 0), (far_omega, 3), (from_sibling, om_near_sib), (gather_on, 0), (pass_omega, 2), (product, 1),
-        (eta_to_near, 0), (far_omega, 1), (eta_to_far, 0), (gather_on, 1), (near_left,), (weigh, 0), (from_sibling, om_far_sib), (product, 2),
-        (merge_on, 0), (weigh, 1), (eta_to_near, 2), (opposite_omega, 3), (gather_on, 2), (eta_to_near, 1), (opposite_omega, 1), (opposite_omega, 2),
-        (opposite_omega, 0), (from_sibling, om_opp_sib), (product, 3), (eta_to_far, 1), (near_eta,), (eta_pass, 1), (eta_pass, 0), (share_near_eta,),
-        (merge_on, 1), (first_term, rows), (gather_on, 3), (eta_to_far, 3), (weigh, 2), (eta_pass, 3), (first_term, 0), (share_eta, 1),
-        (eta_to_far, 2), (eta_pass, 2), (own_left,), (settle_eta,), (share_eta, 0), (finish, 0), (weigh, 3), (last_term, 0), (share_eta, 3),
-        (last_term, 1), (merge_on, 2), (share_eta, 2), (finish, 1), (last_term, 3), (merge_on, 3), (last_term, 2), (finish, 2), (finish, 3),
-        (swapped, 2), (swapped, 1), (swapped, 3), (swapped, 0),
+        (recouple,), (own_omega,), (recouple_back,), (omega_to_far, 2), (near_omega, 2), (omega_to_far, 1), (omega_to_far, 3), (meet,),
+        (near_omega, 1), (near_omega, 0), (product, 0), (near_omega, 3), (omega_to_far, 0), (gather_on, 0), (pass_omega, 1),
+        (from_sibling, om_near_sib), (pass_omega, 0), (pass_omega, 3), (product, 1), (set_weights,), (gather_on, 1), (far_omega, 2), (pass_omega, 2),
+        (weigh, 0), (far_omega, 1), (far_omega, 3), (far_omega, 0), (weigh, 1), (eta_to_near, 1), (from_sibling, om_far_sib), (product, 2),
+        (opposite_omega, 1), (opposite_omega, 0), (own_left,), (merge_on, 0), (opposite_omega, 3), (eta_to_near, 2), (opposite_omega, 2),
+        (eta_to_near, 0), (gather_on, 2), (eta_to_near, 3), (merge_on, 1), (from_sibling, om_opp_sib), (product, 3), (near_left,), (finish, 0),
+        (first_term, 0), (eta_to_far, 0), (finish, 1), (eta_to_far, 1), (gather_on, 3), (weigh, 2), (near_eta,), (eta_pass, 0), (share_near_eta,),
+        (eta_pass, 2), (eta_to_far, 2), (weigh, 3), (eta_pass, 1), (first_term, rows), (share_eta, 0), (eta_to_far, 3), (settle_eta,),
+        (share_eta, 2), (eta_pass, 3), (merge_on, 2), (share_eta, 1), (last_term, 0), (merge_on, 3), (last_term, 2), (share_eta, 3), (last_term, 1),
+        (swapped, 0), (last_term, 3), (finish, 2), (finish, 3), (swapped, 2), (swapped, 1), (swapped, 3),
     ]
     for step, *which in plan:
         step(*which)
@@ -353,6 +385,8 @@
             pltpu.SemaphoreType.DMA((COPIES,)),
             pltpu.SemaphoreType.DMA((COPIES,)),
             pltpu.SemaphoreType.DMA((32,)),
+            pltpu.SemaphoreType.REGULAR,
+            pltpu.SemaphoreType.REGULAR,
         ],
         compiler_params=pltpu.CompilerParams(collective_id=0, has_side_effects=True, vmem_limit_bytes=60 * 1024 * 1024),
         cost_estimate=pl.CostEstimate(flops=10 * rows * width * width, bytes_accessed=14 * rows * width * 2, transcendentals=0),

time: 86.6 us -> 85.9 us (level)
  the two profiles are of different devices: /device:TPU:1 before, /device:TPU:17 now
where the time goes in v3:
time: 85.9 us; the launch traced here: 85.8 us
  Pallas kernels  82.5 us (96%)
  local copies, waits for them, and re-layouts  1.94 us (2%)
  between operations  1.29 us (2%)
    pallas_call x1, Pallas kernels, body(): pl.pallas_call(kernel, out_shape=(out, out), in_specs=[smem] * 3 + [any_s...  82.5 us
    unnamed x2, local copies, waits for them, and re-layouts  1.94 us

profile of v3, /device:TPU:17, one launch (start us, length us, event | category | flops | bytes accessed | tf_op | source)
XLA Modules:
  0.0 85.8 jit_solution(6285603157361963623)
XLA Ops:
  1.3 82.5 %commutators.1 = (bf16[256,2048]{1,0:T(8,128)(2,1)S(1)}, bf16[256,2048]{1,0:T(8,128)(2,1)S(1)}) custom-call(s32[1]{0:T(128)S(6)} %copy.12.states_ref, s32[1,8]{1,0:T(1,128)} %map_ref.1, f32[1,8]{1,0:T(1,128)} %coef_ref.1, bf16[256,2048]{1,0:T(8,128)(2,1)} %bitcast.8, bf16[256,2048]{1,0:T(8,128)(2,1)} %bitcast.9, bf16[2048,2048]{1,0:T(8,128)(2,1)} %bitcast.7), custom_call_target="tpu_custom_call" | custom-call | flops 10737418240 | bytes 14680064 | tf_op jit(solution)/shard_map/commutators/pallas_call | solution.py:359
  83.8 1.0 %copy.10 = bf16[1,256,2048]{2,1,0:T(8,128)(2,1)} copy(bf16[1,256,2048]{2,1,0:T(8,128)(2,1)S(1)} %bitcast.6) | data formatting | bytes 2097152
  84.8 1.0 %copy.11 = bf16[1,256,2048]{2,1,0:T(8,128)(2,1)} copy(bf16[1,256,2048]{2,1,0:T(8,128)(2,1)S(1)} %bitcast.5) | data formatting | bytes 2097152

commit v4 on v3

--- a/solution.py
+++ b/solution.py
@@ -14,7 +14,7 @@
 NT = (((1,), (1,)), ((), ()))
 SIDE = 4
 PIECES = 4
-COPIES = 128
+COPIES = 160
 
 
 def dot(a, b, dims):
@@ -180,55 +180,71 @@
 
     step0 = 1 - 2 * (x % 2)
     chips = [(x, x), ((x + step0 + SIDE) % SIDE, (x - step0 + SIDE) % SIDE), ((x - step0 + SIDE) % SIDE, (x + step0 + SIDE) % SIDE), (xo, xo)]
+    parts_of = [(0, 0, rows), (1, 0, rows), (2, 0, rows), (3, 0, rows // 2), (3, rows // 2, rows // 2)]
     quads = {}
 
+    def start_of(p, m):
+        k, lo, _ = parts_of[p]
+        return pl.multiple_of((chips[k][m] * 2 + m) * rows + lo, 128)
+
+    def cut(ref, p, *index):
+        k, lo, size = parts_of[p]
+        return ref.at[index[0], k, *index[1:], :, pl.ds(lo, size)]
+
     def product(p):
-        for m in range(2):
-            first = pl.multiple_of((chips[p][m] * 2 + m) * rows, 128)
-            part = dot(f_ref[...], om[pl.ds(first, rows), :], NT)
-            keep = lax.broadcasted_iota(jnp.int32, (1, rows), 1) + first < live
-            gath[m, p, 0] = jnp.where(keep, part, 0.0).astype(BF)
-            ahead = send(gath.at[m, p, 0], gath.at[m, p, 1], moves[m](turn))
-            back = send(gath.at[m, p, 0], gath.at[m, p, 2], moves[m](-turn))
+        size = parts_of[p][2]
+        if p >= 3:
+            for r in range((p - 3) * 2, (p - 3) * 2 + 2):
+                om_opp_sib[r].wait_recv()
+        for m in range(2):
+            first = start_of(p, m)
+            part = dot(f_ref[...], om[pl.ds(first, size), :], NT)
+            keep = lax.broadcasted_iota(jnp.int32, (1, size), 1) + first < live
+            cut(gath, p, m, 0)[...] = jnp.where(keep, part, 0.0).astype(BF)
+            ahead = send(cut(gath, p, m, 0), cut(gath, p, m, 1), moves[m](turn))
+            back = send(cut(gath, p, m, 0), cut(gath, p, m, 2), moves[m](-turn))
             quads[m, p] = [ahead, back]
 
     def gather_on(p):
         for m in range(2):
             quads[m, p][0].wait_recv()
-            quads[m, p].append(send(gath.at[m, p, 1], gath.at[m, p, 3], moves[m](turn)))
+            quads[m, p].append(send(cut(gath, p, m, 1), cut(gath, p, m, 3), moves[m](turn)))
 
     def weigh(p):
         for m in range(2):
             quads[m, p][1].wait_recv()
             quads[m, p][2].wait_recv()
 
-            def step(i, carry, m=m):
+            k, lo, size = parts_of[p]
+            cols = pl.ds(lo, size)
+
+            def step(i, carry, m=m, k=k, cols=cols, size=size):
                 at_rows = pl.ds(pl.multiple_of(i * sub, 16), sub)
-                parts = [gath[m, p, s, at_rows, :].astype(F32) for s in range(4)]
+                parts = [gath[m, k, s, at_rows, cols].astype(F32) for s in range(4)]
                 for t, out in enumerate((own_sum, sum_next, sum_prev, sum_two)):
-                    total = sum(wvec[m * 16 + t * 4 + s : m * 16 + t * 4 + s + 1, :] * parts[s] for s in range(4))
-                    out[m, p, at_rows, :] = total.astype(out.dtype)
+                    total = sum(wvec[m * 16 + t * 4 + s : m * 16 + t * 4 + s + 1, 0:size] * parts[s] for s in range(4))
+                    out[m, k, at_rows, cols] = total.astype(out.dtype)
                 return carry
 
             lax.fori_loop(0, PIECES, step, 0)
             other = moves[1 - m]
-            two = send(sum_two.at[m, p], merge.at[m, p], other(turn))
-            prev = send(sum_prev.at[m, p], fin_a.at[m, p], other(-turn))
+            two = send(cut(sum_two, p, m), cut(merge, p, m), other(turn))
+            prev = send(cut(sum_prev, p, m), cut(fin_a, p, m), other(-turn))
             quads[m, p] += [two, prev]
 
     def merge_on(p):
         for m in range(2):
             quads[m, p][3].wait_recv()
-            sum_next[m, p] = (sum_next[m, p].astype(F32) + merge[m, p].astype(F32)).astype(BF)
-            quads[m, p].append(send(sum_next.at[m, p], fin_b.at[m, p], moves[1 - m](turn)))
+            ahead = cut(sum_next, p, m)
+            ahead[...] = (ahead[...].astype(F32) + cut(merge, p, m)[...].astype(F32)).astype(BF)
+            quads[m, p].append(send(ahead, cut(fin_b, p, m), moves[1 - m](turn)))
 
     def finish(p):
         for m in range(2):
             quads[m, p][4].wait_recv()
             quads[m, p][5].wait_recv()
-            total = own_sum[m, p] + fin_a[m, p].astype(F32) + fin_b[m, p].astype(F32)
-            first = pl.multiple_of((chips[p][m] * 2 + m) * rows, 128)
-            cross_ref[:, pl.ds(first, rows)] = total.astype(BF)
+            total = cut(own_sum, p, m)[...] + cut(fin_a, p, m)[...].astype(F32) + cut(fin_b, p, m)[...].astype(F32)
+            cross_ref[:, pl.ds(start_of(p, m), parts_of[p][2])] = total.astype(BF)
 
     def recouple():
         get_eta.wait()
@@ -274,7 +290,9 @@
     eta_n, eta_f, eta_on, eta_f_sib, eta_o_sib, eta_n_sib, own_copy = {}, {}, {}, {}, {}, [], []
 
     def eta_to_near(r):
-        eta_n[r] = send(eta_hbm.at[pl.ds(r * sub, sub)], eta_near.at[pl.ds(r * sub, sub)], near)
+        side, first = (h, r) if r < 2 else (hf, r - 2)
+        cols = pl.ds(pl.multiple_of(side * half + first * 2 * quarter, 128), 2 * quarter)
+        eta_n[r] = send(eta_hbm.at[:, cols], eta_near.at[:, cols], near)
 
     def eta_cols(q, side):
         return pl.ds(pl.multiple_of(side * half + q * quarter, 128), quarter)
@@ -292,9 +310,8 @@
             cols = pl.ds(pl.multiple_of(h * half + t * 512, 128), 512)
             acc[lo : lo + rows, t * 512 : (t + 1) * 512] = dot(eta_left[lo : lo + rows, :], om[:, cols], NN)
 
-    def near_eta():
-        for r in range(PIECES):
-            eta_n[r].wait_recv()
+    def near_eta(r):
+        eta_n[r].wait_recv()
 
     def share_near_eta():
         eta_n_sib.append(send(eta_near.at[:, half_cols], at(eta_half, theirs_n, rows), sib))
@@ -332,16 +349,17 @@
         swaps[q].wait_recv()
 
     plan = [
-        (recouple,), (own_omega,), (recouple_back,), (omega_to_far, 2), (near_omega, 2), (omega_to_far, 1), (omega_to_far, 3), (meet,),
-        (near_omega, 1), (near_omega, 0), (product, 0), (near_omega, 3), (omega_to_far, 0), (gather_on, 0), (pass_omega, 1),
-        (from_sibling, om_near_sib), (pass_omega, 0), (pass_omega, 3), (product, 1), (set_weights,), (gather_on, 1), (far_omega, 2), (pass_omega, 2),
-        (weigh, 0), (far_omega, 1), (far_omega, 3), (far_omega, 0), (weigh, 1), (eta_to_near, 1), (from_sibling, om_far_sib), (product, 2),
-        (opposite_omega, 1), (opposite_omega, 0), (own_left,), (merge_on, 0), (opposite_omega, 3), (eta_to_near, 2), (opposite_omega, 2),
-        (eta_to_near, 0), (gather_on, 2), (eta_to_near, 3), (merge_on, 1), (from_sibling, om_opp_sib), (product, 3), (near_left,), (finish, 0),
-        (first_term, 0), (eta_to_far, 0), (finish, 1), (eta_to_far, 1), (gather_on, 3), (weigh, 2), (near_eta,), (eta_pass, 0), (share_near_eta,),
-        (eta_pass, 2), (eta_to_far, 2), (weigh, 3), (eta_pass, 1), (first_term, rows), (share_eta, 0), (eta_to_far, 3), (settle_eta,),
-        (share_eta, 2), (eta_pass, 3), (merge_on, 2), (share_eta, 1), (last_term, 0), (merge_on, 3), (last_term, 2), (share_eta, 3), (last_term, 1),
-        (swapped, 0), (last_term, 3), (finish, 2), (finish, 3), (swapped, 2), (swapped, 1), (swapped, 3),
+        (recouple,), (meet,), (own_omega,), (own_left,), (omega_to_far, 1), (recouple_back,), (omega_to_far, 0), (product, 0), (omega_to_far, 3),
+        (omega_to_far, 2), (near_omega, 2), (near_omega, 3), (pass_omega, 3), (near_omega, 0), (near_omega, 1), (gather_on, 0), (pass_omega, 1),
+        (from_sibling, om_near_sib), (set_weights,), (pass_omega, 0), (product, 1), (weigh, 0), (far_omega, 0), (far_omega, 2), (gather_on, 1),
+        (far_omega, 3), (pass_omega, 2), (merge_on, 0), (far_omega, 1), (eta_to_near, 0), (weigh, 1), (eta_to_near, 3), (opposite_omega, 0),
+        (eta_to_far, 1), (from_sibling, om_far_sib), (opposite_omega, 3), (opposite_omega, 1), (product, 2), (product, 3), (eta_to_near, 2),
+        (eta_to_near, 1), (near_left,), (merge_on, 1), (opposite_omega, 2), (near_eta, 0), (gather_on, 2), (product, 4), (gather_on, 3),
+        (first_term, 0), (eta_pass, 0), (eta_pass, 1), (eta_to_far, 0), (gather_on, 4), (weigh, 3), (near_eta, 1), (near_eta, 3), (near_eta, 2),
+        (eta_pass, 3), (weigh, 2), (share_near_eta,), (eta_to_far, 3), (weigh, 4), (share_eta, 0), (eta_pass, 2), (finish, 0), (eta_to_far, 2),
+        (share_eta, 1), (first_term, rows), (settle_eta,), (last_term, 0), (share_eta, 3), (merge_on, 3), (last_term, 1), (share_eta, 2),
+        (merge_on, 4), (merge_on, 2), (last_term, 3), (last_term, 2), (finish, 3), (finish, 1), (finish, 4), (swapped, 1), (swapped, 3), (finish, 2),
+        (swapped, 0), (swapped, 2),
     ]
     for step, *which in plan:
         step(*which)

time: 85.9 us -> 82.2 us (0.957)
  the two profiles are of different devices: /device:TPU:17 before, /device:TPU:1 now
where the time goes in v4:
time: 82.2 us; the launch traced here: 80.9 us
  Pallas kernels  77.7 us (95%)
  local copies, waits for them, and re-layouts  1.94 us (2%)
  between operations  1.29 us (2%)
    pallas_call x1, Pallas kernels, body(): pl.pallas_call(kernel, out_shape=(out, out), in_specs=[smem] * 3 + [any_s...  77.7 us
    unnamed x2, local copies, waits for them, and re-layouts  1.94 us

profile of v4, /device:TPU:1, one launch (start us, length us, event | category | flops | bytes accessed | tf_op | source)
XLA Modules:
  0.0 80.9 jit_solution(1658014870275259081)
XLA Ops:
  1.3 77.7 %commutators.1 = (bf16[256,2048]{1,0:T(8,128)(2,1)S(1)}, bf16[256,2048]{1,0:T(8,128)(2,1)S(1)}) custom-call(s32[1]{0:T(128)S(6)} %copy.12.states_ref, s32[1,8]{1,0:T(1,128)} %map_ref.1, f32[1,8]{1,0:T(1,128)} %coef_ref.1, bf16[256,2048]{1,0:T(8,128)(2,1)} %bitcast.8, bf16[256,2048]{1,0:T(8,128)(2,1)} %bitcast.9, bf16[2048,2048]{1,0:T(8,128)(2,1)} %bitcast.7), custom_call_target="tpu_custom_call" | custom-call | flops 10737418240 | bytes 14680064 | tf_op jit(solution)/shard_map/commutators/pallas_call | solution.py:377
  79.0 1.0 %copy.10 = bf16[1,256,2048]{2,1,0:T(8,128)(2,1)} copy(bf16[1,256,2048]{2,1,0:T(8,128)(2,1)S(1)} %bitcast.6) | data formatting | bytes 2097152
  79.9 1.0 %copy.11 = bf16[1,256,2048]{2,1,0:T(8,128)(2,1)} copy(bf16[1,256,2048]{2,1,0:T(8,128)(2,1)S(1)} %bitcast.5) | data formatting | bytes 2097152

commit v5 on v4

--- a/solution.py
+++ b/solution.py
@@ -361,9 +361,23 @@
         (merge_on, 4), (merge_on, 2), (last_term, 3), (last_term, 2), (finish, 3), (finish, 1), (finish, 4), (swapped, 1), (swapped, 3), (finish, 2),
         (swapped, 0), (swapped, 2),
     ]
+    settled, earlier = 0, {}
     for step, *which in plan:
+        upto = settled
+        if (step, *which) in ((near_eta, 0), (weigh, 4)):
+            upto = earlier.get(step, 0)
+        elif step is swapped and "end" not in earlier:
+            earlier["end"] = True
+            upto = len(started) - 6
+        for copy in started[settled:upto]:
+            copy.wait_send()
+        settled = max(settled, upto)
+        if (step, *which) == (product, 2):
+            earlier[near_eta] = len(started)
+        if (step, *which) == (near_eta, 0):
+            earlier[weigh] = len(started)
         step(*which)
-    for copy in started:
+    for copy in started[settled:]:
         copy.wait_send()
 
 

time: 82.2 us -> 81.6 us (level)
  no operation moved by 1% of the time
where the time goes in v5:
time: 81.6 us; the launch traced here: 80.9 us
  Pallas kernels  77.7 us (95%)
  local copies, waits for them, and re-layouts  1.94 us (2%)
  between operations  1.29 us (2%)
    pallas_call x1, Pallas kernels, body(): pl.pallas_call(kernel, out_shape=(out, out), in_specs=[smem] * 3 + [any_s...  77.7 us
    unnamed x2, local copies, waits for them, and re-layouts  1.94 us

profile of v5, /device:TPU:1, one launch (start us, length us, event | category | flops | bytes accessed | tf_op | source)
XLA Modules:
  0.0 80.9 jit_solution(608110132451637952)
XLA Ops:
  1.3 77.7 %commutators.1 = (bf16[256,2048]{1,0:T(8,128)(2,1)S(1)}, bf16[256,2048]{1,0:T(8,128)(2,1)S(1)}) custom-call(s32[1]{0:T(128)S(6)} %copy.12.states_ref, s32[1,8]{1,0:T(1,128)} %map_ref.1, f32[1,8]{1,0:T(1,128)} %coef_ref.1, bf16[256,2048]{1,0:T(8,128)(2,1)} %bitcast.8, bf16[256,2048]{1,0:T(8,128)(2,1)} %bitcast.9, bf16[2048,2048]{1,0:T(8,128)(2,1)} %bitcast.7), custom_call_target="tpu_custom_call" | custom-call | flops 10737418240 | bytes 14680064 | tf_op jit(solution)/shard_map/commutators/pallas_call | solution.py:391
  79.0 1.0 %copy.10 = bf16[1,256,2048]{2,1,0:T(8,128)(2,1)} copy(bf16[1,256,2048]{2,1,0:T(8,128)(2,1)S(1)} %bitcast.6) | data formatting | bytes 2097152
  80.0 1.0 %copy.11 = bf16[1,256,2048]{2,1,0:T(8,128)(2,1)} copy(bf16[1,256,2048]{2,1,0:T(8,128)(2,1)S(1)} %bitcast.5) | data formatting | bytes 2097152

commit v6 on v5

--- a/solution.py
+++ b/solution.py
@@ -356,9 +356,9 @@
         (eta_to_far, 1), (from_sibling, om_far_sib), (opposite_omega, 3), (opposite_omega, 1), (product, 2), (product, 3), (eta_to_near, 2),
         (eta_to_near, 1), (near_left,), (merge_on, 1), (opposite_omega, 2), (near_eta, 0), (gather_on, 2), (product, 4), (gather_on, 3),
         (first_term, 0), (eta_pass, 0), (eta_pass, 1), (eta_to_far, 0), (gather_on, 4), (weigh, 3), (near_eta, 1), (near_eta, 3), (near_eta, 2),
-        (eta_pass, 3), (weigh, 2), (share_near_eta,), (eta_to_far, 3), (weigh, 4), (share_eta, 0), (eta_pass, 2), (finish, 0), (eta_to_far, 2),
+        (eta_pass, 3), (weigh, 2), (share_near_eta,), (finish, 1), (eta_to_far, 3), (weigh, 4), (share_eta, 0), (eta_pass, 2), (finish, 0), (eta_to_far, 2),
         (share_eta, 1), (first_term, rows), (settle_eta,), (last_term, 0), (share_eta, 3), (merge_on, 3), (last_term, 1), (share_eta, 2),
-        (merge_on, 4), (merge_on, 2), (last_term, 3), (last_term, 2), (finish, 3), (finish, 1), (finish, 4), (swapped, 1), (swapped, 3), (finish, 2),
+        (merge_on, 4), (merge_on, 2), (last_term, 3), (last_term, 2), (finish, 3), (finish, 4), (swapped, 1), (swapped, 3), (finish, 2),
         (swapped, 0), (swapped, 2),
     ]
     settled, earlier = 0, {}

time: 81.6 us -> 81.6 us (level)
  no operation moved by 1% of the time
where the time goes in v6:
time: 81.6 us; the launch traced here: 80.9 us
  Pallas kernels  77.7 us (95%)
  local copies, waits for them, and re-layouts  1.94 us (2%)
  between operations  1.29 us (2%)
    pallas_call x1, Pallas kernels, body(): pl.pallas_call(kernel, out_shape=(out, out), in_specs=[smem] * 3 + [any_s...  77.7 us
    unnamed x2, local copies, waits for them, and re-layouts  1.94 us

profile of v6, /device:TPU:1, one launch (start us, length us, event | category | flops | bytes accessed | tf_op | source)
XLA Modules:
  0.0 80.9 jit_solution(704945131529551901)
XLA Ops:
  1.3 77.7 %commutators.1 = (bf16[256,2048]{1,0:T(8,128)(2,1)S(1)}, bf16[256,2048]{1,0:T(8,128)(2,1)S(1)}) custom-call(s32[1]{0:T(128)S(6)} %copy.12.states_ref, s32[1,8]{1,0:T(1,128)} %map_ref.1, f32[1,8]{1,0:T(1,128)} %coef_ref.1, bf16[256,2048]{1,0:T(8,128)(2,1)} %bitcast.8, bf16[256,2048]{1,0:T(8,128)(2,1)} %bitcast.9, bf16[2048,2048]{1,0:T(8,128)(2,1)} %bitcast.7), custom_call_target="tpu_custom_call" | custom-call | flops 10737418240 | bytes 14680064 | tf_op jit(solution)/shard_map/commutators/pallas_call | solution.py:391
  79.0 1.0 %copy.10 = bf16[1,256,2048]{2,1,0:T(8,128)(2,1)} copy(bf16[1,256,2048]{2,1,0:T(8,128)(2,1)S(1)} %bitcast.6) | data formatting | bytes 2097152
  80.0 1.0 %copy.11 = bf16[1,256,2048]{2,1,0:T(8,128)(2,1)} copy(bf16[1,256,2048]{2,1,0:T(8,128)(2,1)S(1)} %bitcast.5) | data formatting | bytes 2097152
